TPU v7x, 32 devices: a whole 2x2x4 slice. The times are simulated.
32 devices in a mesh: cfg: 2 (over y), tm: 4 (over z), col: 2 (over x), mom: 2 (over core).
Axes of the slice: x: 2, y: 2, z: 4, core: 2. Of those that a mesh axis runs over, the one named last changes fastest.
Arguments:
- prop_src: bfloat16 [8, 2, 2, 512, 512], P(('cfg', 'tm'), None, None, None, 'col'), parts along dimension 0, may hold values from -6 to 6
- prop_sink: bfloat16 [8, 2, 512, 512], P(('cfg', 'tm'), None, None, 'col'), parts along dimension 0, may hold values from -0.1875 to 0.1875
- elemental: bfloat16 [8, 2, 2, 128, 128], P(('cfg', 'tm')), parts along dimension 0, may hold values from -0.375 to 0.375
- op_mom: int32 [8], P('mom'), may hold values from 0 to 1
- op_gamma: int32 [8], P('mom'), may hold values from 0 to 15
Outputs:
- three_point: bfloat16 [8, 2, 8, 2, 512, 512], P(('cfg', 'tm'), None, 'mom', None, None, 'col'), parts along dimension 0
There are 2 independent parts, one for each index of `cfg`. A program takes and returns all parts, laid end to end along the dimension named above; an argument that names none is the same for every part. Nothing has to cross between parts.
All inputs are finite; a program needn't handle non-finite values.
Results may differ from a plain program's by a relative error of at most 0.005.
Values may be sent and summed in bfloat16 or wider, within the bound.
No kernel may reach another device: no remote copies, remote signals or barrier semaphores. Data moves between devices by JAX's collectives and lax.ppermute only.
A program may use at most 64 MiB of HBM per device.

v0:
```python
import functools

import jax
import jax.numpy as jnp
import numpy as np
from jax import lax
from jax.experimental import pallas as pl
from jax.experimental.pallas import tpu as pltpu
from jax.sharding import PartitionSpec as P

bf16 = jnp.bfloat16
f32 = jnp.float32
LIMIT = 16 * 2**20


def gamma_codes():
    one = np.array([[0, 0, 0, 1j], [0, 0, 1j, 0], [0, -1j, 0, 0], [-1j, 0, 0, 0]])
    two = np.array([[0, 0, 0, -1], [0, 0, 1, 0], [0, 1, 0, 0], [-1, 0, 0, 0]], dtype=complex)
    three = np.array([[0, 0, 1j, 0], [0, 0, 0, -1j], [-1j, 0, 0, 0], [0, 1j, 0, 0]])
    four = np.array([[0, 0, 1, 0], [0, 0, 0, 1], [1, 0, 0, 0], [0, 1, 0, 0]], dtype=complex)
    codes = []
    for number in range(16):
        product = np.eye(4, dtype=complex)
        for position, factor in enumerate((one, two, three, four)):
            if number >> position & 1:
                product = product @ factor
        flip = int(np.nonzero(product[0])[0][0])
        code = flip
        for s in range(4):
            assert np.count_nonzero(product[s]) == 1
            power = [p for p in range(4) if product[s, s ^ flip] == (1, 1j, -1, -1j)[p]]
            code |= power[0] << (2 + 2 * s)
        codes.append(code)
    return codes


CODES = gamma_codes()


def turn_kernel(sink_ref, message, sink, sem):
    first = pltpu.make_async_copy(sink_ref.at[0, lax.axis_index("mom")], sink, sem)
    first.start()
    first.wait()
    message[...] = sink[...].T


def turned(prop_sink):
    rows, columns = prop_sink.shape[2:]
    return pl.pallas_call(
        turn_kernel,
        out_shape=jax.ShapeDtypeStruct((columns, rows), bf16),
        in_specs=[pl.BlockSpec(memory_space=pl.ANY)],
        out_specs=pl.BlockSpec(memory_space=pltpu.VMEM),
        scratch_shapes=[pltpu.VMEM((rows, columns), bf16), pltpu.SemaphoreType.DMA],
        compiler_params=pltpu.CompilerParams(vmem_limit_bytes=LIMIT),
        name="turned",
    )(prop_sink)


def lay_kernel(after_ref, elem_ref, message, elem, sems):
    del after_ref
    part = lax.axis_index("mom")
    copies = [pltpu.make_async_copy(elem_ref.at[0, m, part], elem.at[m], sems.at[m]) for m in range(elem.shape[0])]
    for copy in copies:
        copy.start()
    for m, copy in enumerate(copies):
        copy.wait()
        for h in range(2):
            message[:, (2 * m + h) * 128 : (2 * m + h + 1) * 128] = elem[m, h * 64 : h * 64 + 64, :]


def laid(elemental, after):
    moms, ev = elemental.shape[1], elemental.shape[3]
    return pl.pallas_call(
        lay_kernel,
        out_shape=jax.ShapeDtypeStruct((64, 2 * moms * ev), bf16),
        in_specs=[pl.BlockSpec(memory_space=pl.ANY)] * 2,
        out_specs=pl.BlockSpec(memory_space=pltpu.VMEM),
        scratch_shapes=[pltpu.VMEM((moms, ev, ev), bf16), pltpu.SemaphoreType.DMA((moms,))],
        compiler_params=pltpu.CompilerParams(vmem_limit_bytes=LIMIT),
        name="laid",
    )(after, elemental)


def fetch_kernel(mom_ref, gamma_ref, prop_ref, *refs):
    *props, picks, sems = refs
    copies = [pltpu.make_async_copy(prop_ref.at[0, slot], prop, sems.at[slot]) for slot, prop in enumerate(props)]
    for copy in copies:
        copy.start()
    for o in range(mom_ref.shape[0]):
        code = jnp.int32(0)
        for g in range(16):
            code = jnp.where(gamma_ref[o] == g, jnp.int32(CODES[g]), code)
        picks[0, o] = mom_ref[o]
        picks[1, o] = code
    for copy in copies:
        copy.wait()


def fetch(op_mom, op_gamma, prop_src):
    slots, parts, rows, width = prop_src.shape[1:]
    ops = op_mom.shape[0]
    vmem_spec = pl.BlockSpec(memory_space=pltpu.VMEM)
    smem_spec = pl.BlockSpec(memory_space=pltpu.SMEM)
    return pl.pallas_call(
        fetch_kernel,
        out_shape=[jax.ShapeDtypeStruct((parts, rows, width), bf16)] * slots + [jax.ShapeDtypeStruct((2, ops), jnp.int32)],
        in_specs=[smem_spec, smem_spec, pl.BlockSpec(memory_space=pltpu.HBM)],
        out_specs=[vmem_spec] * slots + [smem_spec],
        scratch_shapes=[pltpu.SemaphoreType.DMA((slots,))],
        compiler_params=pltpu.CompilerParams(vmem_limit_bytes=LIMIT),
        name="fetch",
    )(op_mom, op_gamma, prop_src)


def joined(refs):
    return jnp.concatenate([ref[...] for ref in refs], axis=0)


def mixed_kernel(picks, mine_ref, *refs):
    *others, prop, mixed, spins, chosen, chosen_sem = refs
    fetched = pltpu.make_async_copy(picks, chosen, chosen_sem)
    fetched.start()
    moms = spins.shape[0]
    width = prop.shape[2]
    real_first = lax.axis_index("mom") == 0

    def elementals(rows, m):
        return jnp.concatenate([rows[:, (2 * m + h) * 128 : (2 * m + h + 1) * 128] for h in range(2)], axis=0)

    mine = mine_ref[width : width + 64, :]
    other = joined(others)[width : width + 64, :]

    lefts = []
    for m in range(moms):
        one, two = elementals(mine, m), elementals(other, m)
        phi_real = jnp.where(real_first, one, two)
        phi_imag = jnp.where(real_first, two, one)
        lefts.append(jnp.concatenate([phi_real, -phi_imag], axis=1))
        lefts.append(jnp.concatenate([phi_imag, phi_real], axis=1))
    left = jnp.concatenate(lefts, axis=0)
    for s in range(4):
        right = jnp.concatenate([prop[0, s * 128 : s * 128 + 128, :], prop[1, s * 128 : s * 128 + 128, :]], axis=0)
        both = jnp.dot(left, right, preferred_element_type=f32).astype(bf16)
        for m in range(moms):
            real = both[m * 256 : m * 256 + 128]
            imag = both[m * 256 + 128 : m * 256 + 256]
            spins[m, 0, s] = real
            spins[m, 1, s] = -imag
            spins[m, 2, s] = -real
            spins[m, 3, s] = imag

    fetched.wait()
    for o in range(mixed.shape[0]):
        mom = chosen[0, o]
        code = chosen[1, o]
        flip = code & 3
        for s in range(4):
            power = code >> (2 + 2 * s)
            for form, turn in enumerate((0, 3)):
                mixed[o, form, s * 128 : s * 128 + 128, :] = spins[mom, (power + turn) & 3, s ^ flip]


def mixed_blocks(picks, mine, other, prop):
    parts, rows, width = prop.shape
    ops = picks.shape[1]
    moms = 2
    vmem_spec = pl.BlockSpec(memory_space=pltpu.VMEM)
    return pl.pallas_call(
        mixed_kernel,
        out_shape=jax.ShapeDtypeStruct((ops, 2, rows, width), bf16),
        in_specs=[pl.BlockSpec(memory_space=pl.ANY)] + [vmem_spec] * (2 + len(other)),
        out_specs=vmem_spec,
        scratch_shapes=[
            pltpu.VMEM((moms, 4, 4, 128, width), bf16),
            pltpu.SMEM((2, ops), jnp.int32),
            pltpu.SemaphoreType.DMA,
        ],
        compiler_params=pltpu.CompilerParams(vmem_limit_bytes=LIMIT),
        cost_estimate=pl.CostEstimate(flops=1, bytes_accessed=1, transcendentals=0),
        name="mixed",
    )(picks, mine, *other, prop)


def block_kernel(places, cols, counts, *refs):
    groups = []
    for count in counts:
        groups.append(refs[: count + 1])
        refs = refs[count + 1 :]
    mixes = dict(zip(sorted({slot for slot, _ in places}), refs))
    out_ref, made, out_sems = refs[-3:]
    part = lax.axis_index("mom")
    copies = []
    for place, ((slot, hop), (mine, *others)) in enumerate(zip(places, groups)):
        mixed = mixes[slot]
        ops, width = mixed.shape[0], mixed.shape[3]
        source = lax.rem(lax.axis_index("col") + hop, cols)
        ours, theirs = mine[0:width, :], joined(others)[0:width, :]
        sinks = [
            jnp.concatenate([ours, theirs], axis=1),
            jnp.concatenate([jnp.where(part == 0, ours, -ours), jnp.where(part == 0, -theirs, theirs)], axis=1),
        ]
        rows = pl.ds(pl.multiple_of(source * width, width), width)
        for o in range(ops):
            for which in range(2):
                first = part if which == 0 else 1 - part
                right = jnp.concatenate([mixed[o, first], mixed[o, 1 - first]], axis=0)
                made[place, o, which] = jnp.dot(sinks[which], right, preferred_element_type=f32).astype(bf16)
                copies.append(
                    pltpu.make_async_copy(
                        made.at[place, o, which], out_ref.at[0, slot, o, which, rows, :], out_sems.at[place, o, which]
                    )
                )
                copies[-1].start()
    for copy in copies:
        copy.wait()


def blocks(cols, work, mixes, prev, out_shape):
    rows, width = out_shape[4:]
    ops = out_shape[2]
    any_spec = pl.BlockSpec(memory_space=pl.ANY)
    vmem_spec = pl.BlockSpec(memory_space=pltpu.VMEM)
    places = [(slot, hop) for slot, hop, _, _ in work]
    operands = [ref for _, _, mine, others in work for ref in (mine, *others)]
    operands += [mixes[slot] for slot in sorted({slot for slot, _ in places})]
    specs = [vmem_spec] * len(operands)
    aliases = {}
    if prev is not None:
        aliases = {len(operands): 0}
        operands.append(prev)
        specs.append(any_spec)
    return pl.pallas_call(
        functools.partial(block_kernel, places, cols, [len(others) for _, _, _, others in work]),
        out_shape=jax.ShapeDtypeStruct(out_shape, bf16),
        in_specs=specs,
        out_specs=any_spec,
        input_output_aliases=aliases,
        scratch_shapes=[
            pltpu.VMEM((len(places), ops, 2, width, width), bf16),
            pltpu.SemaphoreType.DMA((len(places), ops, 2)),
        ],
        compiler_params=pltpu.CompilerParams(vmem_limit_bytes=LIMIT),
        cost_estimate=pl.CostEstimate(flops=1, bytes_accessed=1, transcendentals=0),
        name="blocks",
    )(*operands)


def signed(block, negative):
    return jnp.where(negative, -block, block)


def half_kernel(mine_ref, mixed, sums):
    part = lax.axis_index("mom")
    for o in range(sums.shape[0]):
        for which in range(2):
            left = mine_ref[...] if which == 0 else signed(mine_ref[...], part == 1)
            first = part if which == 0 else 1 - part
            sums[o, which] = jnp.dot(left, mixed[o, first], preferred_element_type=f32)


def half(mine, mixed):
    ops, width = mixed.shape[0], mixed.shape[3]
    vmem_spec = pl.BlockSpec(memory_space=pltpu.VMEM)
    return pl.pallas_call(
        half_kernel,
        out_shape=jax.ShapeDtypeStruct((ops, 2, width, width), f32),
        in_specs=[vmem_spec] * 2,
        out_specs=vmem_spec,
        compiler_params=pltpu.CompilerParams(vmem_limit_bytes=LIMIT),
        cost_estimate=pl.CostEstimate(flops=1, bytes_accessed=1, transcendentals=0),
        name="half",
    )(mine, mixed)


def rest_kernel(slot, hop, cols, count, *refs):
    others = refs[:count]
    mixed, sums, _, out_ref, made, out_sems = refs[count:]
    ops, width = mixed.shape[0], mixed.shape[3]
    part = lax.axis_index("mom")
    source = lax.rem(lax.axis_index("col") + hop, cols)
    rows = pl.ds(pl.multiple_of(source * width, width), width)
    theirs = joined(others)
    copies = []
    for o in range(ops):
        for which in range(2):
            left = theirs if which == 0 else signed(theirs, part == 0)
            first = part if which == 0 else 1 - part
            block = sums[o, which] + jnp.dot(left, mixed[o, 1 - first], preferred_element_type=f32)
            made[o, which] = block.astype(bf16)
            copies.append(
                pltpu.make_async_copy(made.at[o, which], out_ref.at[0, slot, o, which, rows, :], out_sems.at[o, which])
            )
            copies[-1].start()
    for copy in copies:
        copy.wait()


def rest(slot, hop, cols, others, mixed, sums, prev):
    ops, width = mixed.shape[0], mixed.shape[3]
    any_spec = pl.BlockSpec(memory_space=pl.ANY)
    vmem_spec = pl.BlockSpec(memory_space=pltpu.VMEM)
    return pl.pallas_call(
        functools.partial(rest_kernel, slot, hop, cols, len(others)),
        out_shape=jax.ShapeDtypeStruct(prev.shape, bf16),
        in_specs=[vmem_spec] * (len(others) + 2) + [any_spec],
        out_specs=any_spec,
        input_output_aliases={len(others) + 2: 0},
        scratch_shapes=[pltpu.VMEM((ops, 2, width, width), bf16), pltpu.SemaphoreType.DMA((ops, 2))],
        compiler_params=pltpu.CompilerParams(vmem_limit_bytes=LIMIT),
        cost_estimate=pl.CostEstimate(flops=1, bytes_accessed=1, transcendentals=0),
        name="rest",
    )(*others, mixed, sums, prev)


def on_device(prop_src, prop_sink, elemental, op_mom, op_gamma):
    width = prop_src.shape[4]
    rows = prop_src.shape[3]
    stops = prop_src.shape[1]
    ops = op_mom.shape[0]
    cols = lax.axis_size("col")
    times = lax.axis_size("tm")
    later = [((i + 1) % times, i) for i in range(times)]
    swap = [(0, 1), (1, 0)]
    out_shape = (1, stops, ops, 2, rows, width)
    def swapped(block, pieces):
        cuts = [0, *(block.shape[0] * p // 20 // 16 * 16 for p in pieces), block.shape[0]]
        return [lax.ppermute(block[i:j], "mom", swap) for i, j in zip(cuts, cuts[1:])]

    own = turned(prop_sink)
    moving = [own, laid(elemental, own)]
    out = None
    mixes = {}
    waiting = []
    for slot in range(stops):
        if slot == 0:
            first, second = [lax.ppermute(block, "tm", later) for block in moving]
            *props, picks = fetch(op_mom, op_gamma, prop_src)
            first, props, picks = lax.optimization_barrier((first, props, picks))
            held = jnp.concatenate([first, second])
        else:
            held, out = lax.optimization_barrier((lax.ppermute(held, "tm", later), out))
        other = swapped(held, (6,) if slot == 0 else (6,))
        arrivals = [
            (slot, hop, lax.ppermute(held[:width], "col", [((i + hop) % cols, i) for i in range(cols)]))
            for hop in range(1, cols)
        ]
        mixes[slot] = mixed_blocks(picks, held, other, props[slot])
        out = blocks(cols, waiting + [(slot, 0, held, other)], mixes, out, out_shape)
        waiting = []
        for place, hop, mine in arrivals:
            if slot == stops - 1:
                mine, out = lax.optimization_barrier((mine, out))
            waiting.append((place, hop, mine, swapped(mine, (5,) if slot == 0 else ())))
    for slot, hop, mine, others in waiting:
        out = rest(slot, hop, cols, others, mixes[slot], half(mine, mixes[slot]), out)
    return out


def solution(mesh):
    return jax.shard_map(
        on_device,
        mesh=mesh,
        in_specs=(
            P(("cfg", "tm"), None, None, None, "col"),
            P(("cfg", "tm"), None, None, "col"),
            P(("cfg", "tm"), None, None, None, None),
            P("mom"),
            P("mom"),
        ),
        out_specs=P(("cfg", "tm"), None, "mom", None, None, "col"),
        check_vma=False,
    )
```

profile of v0, /device:TPU:0, one launch (start us, length us, event | category | flops | bytes accessed | tf_op | source)
XLA Modules:
  0.0 35.2 jit_solution(72389576655296378)
XLA Ops:
  0.0 0.0 copy-start.1
  0.0 1.0 %copy-done.1 = bf16[1,2,512,256]{3,2,1,0:T(8,128)(2,1)S(1)} copy-done((bf16[1,2,512,256]{3,2,1,0:T(8,128)(2,1)S(1)}, bf16[1,2,512,256]{3,2,1,0:T(8,128)(2,1)}, u32[]{:S(2)}) %copy-start.1) | copy-done | bytes 524312
  1.0 0.1 turned.1.after_ref
  1.2 5.1 %collective-permute-start = (bf16[256,512]{1,0:T(8,128)(2,1)S(1)}, bf16[256,512]{1,0:T(8,128)(2,1)S(1)}, u32[]{:S(2)}, u32[]{:S(2)}) collective-permute-start(bf16[256,512]{1,0:T(8,128)(2,1)S(1)} %turned.1.after_ref), channel_id=1, source_target_pairs={{4,0},{8,4},{12,8},{0,12},{5,1},{9,5},{13,9},{1,13},{6,2},{10,6},{... | collective-permute-start | bytes 786440 | tf_op jit(solution)/shard_map/ppermute | solution.py:337
  6.3 0.0 copy-start.2
  6.3 0.9 %copy-done.2 = bf16[1,2,2,128,128]{4,3,2,1,0:T(8,128)(2,1)S(1)} copy-done((bf16[1,2,2,128,128]{4,3,2,1,0:T(8,128)(2,1)S(1)}, bf16[1,2,2,128,128]{4,3,2,1,0:T(8,128)(2,1)}, u32[]{:S(2)}) %copy-start.2) | copy-done | bytes 131096
  7.2 0.1 laid.1
  7.3 0.5 %collective-permute-start.1 = (bf16[64,512]{1,0:T(8,128)(2,1)S(1)}, bf16[64,512]{1,0:T(8,128)(2,1)S(1)}, u32[]{:S(2)}, u32[]{:S(2)}) collective-permute-start(bf16[64,512]{1,0:T(8,128)(2,1)S(1)} %laid.1), channel_id=1, source_target_pairs={{4,0},{8,4},{12,8},{0,12},{5,1},{9,5},{13,9},{1,13},{6,2},{10,6},{... | collective-permute-start | bytes 196616 | tf_op jit(solution)/shard_map/ppermute | solution.py:337
  7.8 0.0 copy-start
  7.8 1.2 %copy-done = bf16[1,2,2,512,256]{4,3,2,1,0:T(8,128)(2,1)S(1)} copy-done((bf16[1,2,2,512,256]{4,3,2,1,0:T(8,128)(2,1)S(1)}, bf16[1,2,2,512,256]{4,3,2,1,0:T(8,128)(2,1)}, u32[]{:S(2)}) %copy-start) | copy-done | bytes 1048600
  9.0 0.0 copy-start.3
  9.0 0.7 %copy-done.3 = s32[4]{0:T(128)S(1)} copy-done((s32[4]{0:T(128)S(1)}, s32[4]{0:T(128)}, u32[]{:S(2)}) %copy-start.3) | copy-done | bytes 40
  9.7 0.0 copy-start.4
  9.7 0.7 %copy-done.4 = s32[4]{0:T(128)S(1)} copy-done((s32[4]{0:T(128)S(1)}, s32[4]{0:T(128)}, u32[]{:S(2)}) %copy-start.4) | copy-done | bytes 40
  10.3 1.3 %fetch.1 = (bf16[2,512,256]{2,1,0:T(8,128)(2,1)S(1)}, bf16[2,512,256]{2,1,0:T(8,128)(2,1)S(1)}, s32[2,4]{1,0:T(2,128)S(1)}) custom-call(s32[4]{0:T(128)S(1)} %copy-done.3, s32[4]{0:T(128)S(1)} %copy-done.4, bf16[1,2,2,512,256]{4,3,2,1,0:T(8,128)(2,1)S(1)} %copy-done), custom_call_target="tpu_custom_call" | custom-call | tf_op jit(solution)/shard_map/fetch/pallas_call | solution.py:105
  11.6 0.9 %collective-permute-done = bf16[256,512]{1,0:T(8,128)(2,1)S(1)} collective-permute-done((bf16[256,512]{1,0:T(8,128)(2,1)S(1)}, bf16[256,512]{1,0:T(8,128)(2,1)S(1)}, u32[]{:S(2)}, u32[]{:S(2)}) %collective-permute-start) | collective-permute-done | bytes 262176 | tf_op jit(solution)/shard_map/ppermute | solution.py:337
  12.6 0.7 %collective-permute-done.1 = bf16[64,512]{1,0:T(8,128)(2,1)S(1)} collective-permute-done((bf16[64,512]{1,0:T(8,128)(2,1)S(1)}, bf16[64,512]{1,0:T(8,128)(2,1)S(1)}, u32[]{:S(2)}, u32[]{:S(2)}) %collective-permute-start.1) | collective-permute-done | bytes 65568 | tf_op jit(solution)/shard_map/ppermute | solution.py:337
  13.3 4.3 %collective-permute-start.2 = (bf16[320,512]{1,0:T(8,128)(2,1)S(1)}, bf16[320,512]{1,0:T(8,128)(2,1)S(1)}, u32[]{:S(2)}, u32[]{:S(2)}) collective-permute-start(bf16[320,512]{1,0:T(8,128)(2,1)S(1)} %constant_dynamic-update-slice_fusion.mine_ref.refs_0_), channel_id=1, source_target_pairs={{4,0},{8,4},{12,8},{0,12},{5,1},{9,5},{13,9},{1,13},{6,2},{10,6},{... | collective-permute-start | bytes 983048 | tf_op jit(solution)/shard_map/ppermute | solution.py:342
  17.6 0.1 collective-permute-start.4
  17.7 1.6 %collective-permute-start.6 = (bf16[256,512]{1,0:T(8,128)(2,1)S(1)}, bf16[256,512]{1,0:T(8,128)(2,1)S(1)}, u32[]{:S(2)}, u32[]{:S(2)}) collective-permute-start(bf16[256,512]{1,0:T(8,128)(2,1)S(1)} %collective-permute-done), channel_id=1, source_target_pairs={{2,0},{0,2},{3,1},{1,3},{6,4},{4,6},{7,5},{5,7},{10,8},{8,10},{11,... | collective-permute-start | bytes 786440 | tf_op jit(solution)/shard_map/ppermute | solution.py:345
  19.2 0.2 collective-permute-start.3
  19.4 1.1 %collective-permute-done.3.refs_0_.refs_1_ = bf16[96,512]{1,0:T(8,128)(2,1)S(1)} collective-permute-done((bf16[96,512]{1,0:T(8,128)(2,1)S(1)}, bf16[96,512]{1,0:T(8,128)(2,1)S(1)}, u32[]{:S(2)}, u32[]{:S(2)}) %collective-permute-start.3) | collective-permute-done | bytes 98336 | tf_op jit(solution)/shard_map/ppermute | solution.py:328
  20.6 0.0 collective-permute-done.4.refs_1_.refs_2_
  20.6 0.7 %mixed.2.refs_3_.refs_6_ = bf16[4,2,512,256]{3,2,1,0:T(8,128)(2,1)S(1)} custom-call(s32[2,4]{1,0:T(2,128)S(1)} %get-tuple-element.20.picks, bf16[320,512]{1,0:T(8,128)(2,1)S(1)} %constant_dynamic-update-slice_fusion.mine_ref.refs_0_, bf16[96,512]{1,0:T(8,128)(2,1)S(1)} %collective-permute-done.3.refs_0_.refs_1_, ...), custom_call_target="tpu_custom_call" | custom-call | flops 1 | bytes 1 | tf_op jit(solution)/shard_map/mixed/pallas_call | solution.py:169
  21.3 2.0 %blocks.2.refs_8_ = bf16[1,2,4,2,512,256]{5,4,3,2,1,0:T(8,128)(2,1)} custom-call(bf16[320,512]{1,0:T(8,128)(2,1)S(1)} %constant_dynamic-update-slice_fusion.mine_ref.refs_0_, bf16[96,512]{1,0:T(8,128)(2,1)S(1)} %collective-permute-done.3.refs_0_.refs_1_, bf16[224,512]{1,0:T(8,128)(2,1)S(1)} %collective-permute-done.4.refs_1_.refs_2_, ...), custom_call_target="tpu_custom_call" | custom-call | flops 1 | bytes 1 | tf_op jit(solution)/shard_map/blocks/pallas_call | solution.py:233
  23.4 0.3 collective-permute-done.2.mine_ref.refs_3_
  23.7 1.6 %collective-permute-start.5 = (bf16[256,512]{1,0:T(8,128)(2,1)S(1)}, bf16[256,512]{1,0:T(8,128)(2,1)S(1)}, u32[]{:S(2)}, u32[]{:S(2)}) collective-permute-start(bf16[256,512]{1,0:T(8,128)(2,1)S(1)} %slice.23), channel_id=1, source_target_pairs={{2,0},{0,2},{3,1},{1,3},{6,4},{4,6},{7,5},{5,7},{10,8},{8,10},{11,... | collective-permute-start | bytes 786440 | tf_op jit(solution)/shard_map/ppermute | solution.py:345
  25.3 0.1 collective-permute-start.10
  25.3 1.1 %collective-permute-done.6.refs_0_ = bf16[256,512]{1,0:T(8,128)(2,1)S(1)} collective-permute-done((bf16[256,512]{1,0:T(8,128)(2,1)S(1)}, bf16[256,512]{1,0:T(8,128)(2,1)S(1)}, u32[]{:S(2)}, u32[]{:S(2)}) %collective-permute-start.6) | collective-permute-done | bytes 262176 | tf_op jit(solution)/shard_map/ppermute | solution.py:345
  26.5 0.1 collective-permute-start.8
  26.6 0.5 %collective-permute-start.9 = (bf16[96,512]{1,0:T(8,128)(2,1)S(1)}, bf16[96,512]{1,0:T(8,128)(2,1)S(1)}, u32[]{:S(2)}, u32[]{:S(2)}) collective-permute-start(bf16[96,512]{1,0:T(8,128)(2,1)S(1)} %slice.26), channel_id=1, source_target_pairs={{0,1},{1,0},{2,3},{3,2},{4,5},{5,4},{6,7},{7,6},{8,9},{9,8},{10,11... | collective-permute-start | bytes 294920 | tf_op jit(solution)/shard_map/ppermute | solution.py:328
  27.1 0.1 collective-permute-start.7
  27.2 0.9 %collective-permute-done.9.refs_0_.refs_4_ = bf16[96,512]{1,0:T(8,128)(2,1)S(1)} collective-permute-done((bf16[96,512]{1,0:T(8,128)(2,1)S(1)}, bf16[96,512]{1,0:T(8,128)(2,1)S(1)}, u32[]{:S(2)}, u32[]{:S(2)}) %collective-permute-start.9) | collective-permute-done | bytes 98336 | tf_op jit(solution)/shard_map/ppermute | solution.py:328
  28.1 0.0 collective-permute-done.10.refs_1_.refs_5_
  28.1 0.7 %mixed.3.refs_7_.refs_1_ = bf16[4,2,512,256]{3,2,1,0:T(8,128)(2,1)S(1)} custom-call(s32[2,4]{1,0:T(2,128)S(1)} %get-tuple-element.20.picks, bf16[320,512]{1,0:T(8,128)(2,1)S(1)} %collective-permute-done.2.mine_ref.refs_3_, bf16[96,512]{1,0:T(8,128)(2,1)S(1)} %collective-permute-done.9.refs_0_.refs_4_, ...), custom_call_target="tpu_custom_call" | custom-call | flops 1 | bytes 1 | tf_op jit(solution)/shard_map/mixed/pallas_call | solution.py:169
  28.9 0.0 collective-permute-done.7.refs_1_
  28.9 0.0 collective-permute-done.8.refs_2_
  28.9 3.2 %blocks.3.refs_3_ = bf16[1,2,4,2,512,256]{5,4,3,2,1,0:T(8,128)(2,1)} custom-call(bf16[256,512]{1,0:T(8,128)(2,1)S(1)} %collective-permute-done.6.refs_0_, bf16[64,512]{1,0:T(8,128)(2,1)S(1)} %collective-permute-done.7.refs_1_, bf16[192,512]{1,0:T(8,128)(2,1)S(1)} %collective-permute-done.8.refs_2_, ...), custom_call_target="tpu_custom_call", output_to_operand_aliasing={{}: (8, {})} | custom-call | flops 1 | bytes 1 | tf_op jit(solution)/shard_map/blocks/pallas_call | solution.py:233
  32.1 0.0 collective-permute-done.5.mine_ref
  32.1 0.4 %collective-permute-start.11 = (bf16[256,512]{1,0:T(8,128)(2,1)S(1)}, bf16[256,512]{1,0:T(8,128)(2,1)S(1)}, u32[]{:S(2)}, u32[]{:S(2)}) collective-permute-start(bf16[256,512]{1,0:T(8,128)(2,1)S(1)} %collective-permute-done.5.mine_ref), channel_id=1, source_target_pairs={{0,1},{1,0},{2,3},{3,2},{4,5},{5,4},{6,7},{7,6},{8,9},{9,8},{10,11... | collective-permute-start | bytes 786440 | tf_op jit(solution)/shard_map/ppermute | solution.py:328
  32.5 0.7 %half.1.refs_2_ = f32[4,2,256,256]{3,2,1,0:T(8,128)S(1)} custom-call(bf16[256,512]{1,0:T(8,128)(2,1)S(1)} %collective-permute-done.5.mine_ref, bf16[4,2,512,256]{3,2,1,0:T(8,128)(2,1)S(1)} %mixed.3.refs_7_.refs_1_), custom_call_target="tpu_custom_call" | custom-call | flops 1 | bytes 1 | tf_op jit(solution)/shard_map/half/pallas_call | solution.py:265
  33.2 0.5 %collective-permute-done.11.refs_0_ = bf16[256,512]{1,0:T(8,128)(2,1)S(1)} collective-permute-done((bf16[256,512]{1,0:T(8,128)(2,1)S(1)}, bf16[256,512]{1,0:T(8,128)(2,1)S(1)}, u32[]{:S(2)}, u32[]{:S(2)}) %collective-permute-start.11) | collective-permute-done | bytes 262176 | tf_op jit(solution)/shard_map/ppermute | solution.py:328
  33.7 1.5 %rest.1 = bf16[1,2,4,2,512,256]{5,4,3,2,1,0:T(8,128)(2,1)} custom-call(bf16[256,512]{1,0:T(8,128)(2,1)S(1)} %collective-permute-done.11.refs_0_, bf16[4,2,512,256]{3,2,1,0:T(8,128)(2,1)S(1)} %mixed.3.refs_7_.refs_1_, f32[4,2,256,256]{3,2,1,0:T(8,128)S(1)} %half.1.refs_2_, bf16[1,2,4,2,512,256]{5,4,3,2,1,0:T(8,128)(2,1)} %blocks.3.refs_3_), custom_call_target="tpu_custom_call", output_to_operand_aliasing={{}: (3, {})} | custom-call | flops 1 | bytes 1 | tf_op jit(solution)/shard_map/rest/pallas_call | solution.py:303
  (9 shorter events, 0.1 us)
Async XLA Ops:
  0.0 1.0 %copy-start.1 = (bf16[1,2,512,256]{3,2,1,0:T(8,128)(2,1)S(1)}, bf16[1,2,512,256]{3,2,1,0:T(8,128)(2,1)}, u32[]{:S(2)}) copy-start(bf16[1,2,512,256]{3,2,1,0:T(8,128)(2,1)} %sink_ref.1) | copy-start | bytes 1572868
  1.2 11.4 %collective-permute-start = (bf16[256,512]{1,0:T(8,128)(2,1)S(1)}, bf16[256,512]{1,0:T(8,128)(2,1)S(1)}, u32[]{:S(2)}, u32[]{:S(2)}) collective-permute-start(bf16[256,512]{1,0:T(8,128)(2,1)S(1)} %turned.1.after_ref), channel_id=1, source_target_pairs={{4,0},{8,4},{12,8},{0,12},{5,1},{9,5},{13,9},{1,13},{6,2},{10,6},{... | collective-permute-start | bytes 786440 | tf_op jit(solution)/shard_map/ppermute | solution.py:337
  6.3 0.9 %copy-start.2 = (bf16[1,2,2,128,128]{4,3,2,1,0:T(8,128)(2,1)S(1)}, bf16[1,2,2,128,128]{4,3,2,1,0:T(8,128)(2,1)}, u32[]{:S(2)}) copy-start(bf16[1,2,2,128,128]{4,3,2,1,0:T(8,128)(2,1)} %elem_ref.1) | copy-start | bytes 393220
  7.3 6.0 %collective-permute-start.1 = (bf16[64,512]{1,0:T(8,128)(2,1)S(1)}, bf16[64,512]{1,0:T(8,128)(2,1)S(1)}, u32[]{:S(2)}, u32[]{:S(2)}) collective-permute-start(bf16[64,512]{1,0:T(8,128)(2,1)S(1)} %laid.1), channel_id=1, source_target_pairs={{4,0},{8,4},{12,8},{0,12},{5,1},{9,5},{13,9},{1,13},{6,2},{10,6},{... | collective-permute-start | bytes 196616 | tf_op jit(solution)/shard_map/ppermute | solution.py:337
  7.8 1.2 %copy-start = (bf16[1,2,2,512,256]{4,3,2,1,0:T(8,128)(2,1)S(1)}, bf16[1,2,2,512,256]{4,3,2,1,0:T(8,128)(2,1)}, u32[]{:S(2)}) copy-start(bf16[1,2,2,512,256]{4,3,2,1,0:T(8,128)(2,1)} %prop_ref.1) | copy-start | bytes 3145732
  9.0 0.7 %copy-start.3 = (s32[4]{0:T(128)S(1)}, s32[4]{0:T(128)}, u32[]{:S(2)}) copy-start(s32[4]{0:T(128)} %mom_ref.1) | copy-start | bytes 52
  9.7 0.7 %copy-start.4 = (s32[4]{0:T(128)S(1)}, s32[4]{0:T(128)}, u32[]{:S(2)}) copy-start(s32[4]{0:T(128)} %gamma_ref.1) | copy-start | bytes 52
  13.3 10.4 %collective-permute-start.2 = (bf16[320,512]{1,0:T(8,128)(2,1)S(1)}, bf16[320,512]{1,0:T(8,128)(2,1)S(1)}, u32[]{:S(2)}, u32[]{:S(2)}) collective-permute-start(bf16[320,512]{1,0:T(8,128)(2,1)S(1)} %constant_dynamic-update-slice_fusion.mine_ref.refs_0_), channel_id=1, source_target_pairs={{4,0},{8,4},{12,8},{0,12},{5,1},{9,5},{13,9},{1,13},{6,2},{10,6},{... | collective-permute-start | bytes 983048 | tf_op jit(solution)/shard_map/ppermute | solution.py:342
  17.6 3.0 %collective-permute-start.4 = (bf16[224,512]{1,0:T(8,128)(2,1)S(1)}, bf16[224,512]{1,0:T(8,128)(2,1)S(1)}, u32[]{:S(2)}, u32[]{:S(2)}) collective-permute-start(bf16[224,512]{1,0:T(8,128)(2,1)S(1)} %slice.28), channel_id=1, source_target_pairs={{0,1},{1,0},{2,3},{3,2},{4,5},{5,4},{6,7},{7,6},{8,9},{9,8},{10,11... | collective-permute-start | bytes 688136 | tf_op jit(solution)/shard_map/ppermute | solution.py:328
  17.7 8.8 %collective-permute-start.6 = (bf16[256,512]{1,0:T(8,128)(2,1)S(1)}, bf16[256,512]{1,0:T(8,128)(2,1)S(1)}, u32[]{:S(2)}, u32[]{:S(2)}) collective-permute-start(bf16[256,512]{1,0:T(8,128)(2,1)S(1)} %collective-permute-done), channel_id=1, source_target_pairs={{2,0},{0,2},{3,1},{1,3},{6,4},{4,6},{7,5},{5,7},{10,8},{8,10},{11,... | collective-permute-start | bytes 786440 | tf_op jit(solution)/shard_map/ppermute | solution.py:345
  19.2 1.4 %collective-permute-start.3 = (bf16[96,512]{1,0:T(8,128)(2,1)S(1)}, bf16[96,512]{1,0:T(8,128)(2,1)S(1)}, u32[]{:S(2)}, u32[]{:S(2)}) collective-permute-start(bf16[96,512]{1,0:T(8,128)(2,1)S(1)} %slice.21), channel_id=1, source_target_pairs={{0,1},{1,0},{2,3},{3,2},{4,5},{5,4},{6,7},{7,6},{8,9},{9,8},{10,11... | collective-permute-start | bytes 294920 | tf_op jit(solution)/shard_map/ppermute | solution.py:328
  23.7 8.4 %collective-permute-start.5 = (bf16[256,512]{1,0:T(8,128)(2,1)S(1)}, bf16[256,512]{1,0:T(8,128)(2,1)S(1)}, u32[]{:S(2)}, u32[]{:S(2)}) collective-permute-start(bf16[256,512]{1,0:T(8,128)(2,1)S(1)} %slice.23), channel_id=1, source_target_pairs={{2,0},{0,2},{3,1},{1,3},{6,4},{4,6},{7,5},{5,7},{10,8},{8,10},{11,... | collective-permute-start | bytes 786440 | tf_op jit(solution)/shard_map/ppermute | solution.py:345
  25.3 2.9 %collective-permute-start.10 = (bf16[224,512]{1,0:T(8,128)(2,1)S(1)}, bf16[224,512]{1,0:T(8,128)(2,1)S(1)}, u32[]{:S(2)}, u32[]{:S(2)}) collective-permute-start(bf16[224,512]{1,0:T(8,128)(2,1)S(1)} %slice.27), channel_id=1, source_target_pairs={{0,1},{1,0},{2,3},{3,2},{4,5},{5,4},{6,7},{7,6},{8,9},{9,8},{10,11... | collective-permute-start | bytes 688136 | tf_op jit(solution)/shard_map/ppermute | solution.py:328
  26.5 2.4 %collective-permute-start.8 = (bf16[192,512]{1,0:T(8,128)(2,1)S(1)}, bf16[192,512]{1,0:T(8,128)(2,1)S(1)}, u32[]{:S(2)}, u32[]{:S(2)}) collective-permute-start(bf16[192,512]{1,0:T(8,128)(2,1)S(1)} %slice.30), channel_id=1, source_target_pairs={{0,1},{1,0},{2,3},{3,2},{4,5},{5,4},{6,7},{7,6},{8,9},{9,8},{10,11... | collective-permute-start | bytes 589832 | tf_op jit(solution)/shard_map/ppermute | solution.py:328
  26.6 1.6 %collective-permute-start.9 = (bf16[96,512]{1,0:T(8,128)(2,1)S(1)}, bf16[96,512]{1,0:T(8,128)(2,1)S(1)}, u32[]{:S(2)}, u32[]{:S(2)}) collective-permute-start(bf16[96,512]{1,0:T(8,128)(2,1)S(1)} %slice.26), channel_id=1, source_target_pairs={{0,1},{1,0},{2,3},{3,2},{4,5},{5,4},{6,7},{7,6},{8,9},{9,8},{10,11... | collective-permute-start | bytes 294920 | tf_op jit(solution)/shard_map/ppermute | solution.py:328
  27.1 1.7 %collective-permute-start.7 = (bf16[64,512]{1,0:T(8,128)(2,1)S(1)}, bf16[64,512]{1,0:T(8,128)(2,1)S(1)}, u32[]{:S(2)}, u32[]{:S(2)}) collective-permute-start(bf16[64,512]{1,0:T(8,128)(2,1)S(1)} %slice.29), channel_id=1, source_target_pairs={{0,1},{1,0},{2,3},{3,2},{4,5},{5,4},{6,7},{7,6},{8,9},{9,8},{10,11... | collective-permute-start | bytes 196616 | tf_op jit(solution)/shard_map/ppermute | solution.py:328
  32.1 1.6 %collective-permute-start.11 = (bf16[256,512]{1,0:T(8,128)(2,1)S(1)}, bf16[256,512]{1,0:T(8,128)(2,1)S(1)}, u32[]{:S(2)}, u32[]{:S(2)}) collective-permute-start(bf16[256,512]{1,0:T(8,128)(2,1)S(1)} %collective-permute-done.5.mine_ref), channel_id=1, source_target_pairs={{0,1},{1,0},{2,3},{3,2},{4,5},{5,4},{6,7},{7,6},{8,9},{9,8},{10,11... | collective-permute-start | bytes 786440 | tf_op jit(solution)/shard_map/ppermute | solution.py:328
where the time goes:
time: 35.5 us; the launch traced here: 35.2 us
  starting transfers between devices  14.4 us (41%)
  Pallas kernels  10.4 us (29%)
  waiting for transfers between devices  5.63 us (16%)
  local copies, waits for them, and re-layouts  4.59 us (13%)
    ppermute x2, starting transfers between devices, on_device(): first, second = [lax.ppermute(block, 'tm', later) for block in moving]  5.6 us
    pallas_call x2, Pallas kernels, blocks(): pl.pallas_call(functools.partial(block_kernel, places, cols, [len(others)...  5.26 us
    unnamed x11, local copies, waits for them, and re-layouts  4.5 us
    ppermute x1, starting transfers between devices, on_device(): held, out = lax.optimization_barrier((lax.ppermute(held, 'tm', later), out))  4.28 us
    ppermute x2, starting transfers between devices, on_device(): lax.ppermute(held[:width], 'col', [((i + hop) % cols, i) for i in range(c...  3.11 us
    ppermute x7, waiting for transfers between devices, swapped(): lax.ppermute(block[i:j], 'mom', swap)  2.55 us
    ppermute x2, waiting for transfers between devices, on_device(): first, second = [lax.ppermute(block, 'tm', later) for block in moving]  1.63 us
    pallas_call x1, Pallas kernels, rest(): pl.pallas_call(functools.partial(rest_kernel, slot, hop, cols, len(others...  1.49 us
  transfers between devices with their start and end apart: 12, of which 7 were waited for; matrix products, arithmetic and copies ran while one was open for 0% of the time, Pallas kernels for 25%

commit v1 on v0

--- a/solution.py
+++ b/solution.py
@@ -118,7 +118,7 @@
 
 
 def mixed_kernel(picks, mine_ref, *refs):
-    *others, prop, mixed, spins, chosen, chosen_sem = refs
+    first, prop, mixed, spins, chosen, chosen_sem = refs
     fetched = pltpu.make_async_copy(picks, chosen, chosen_sem)
     fetched.start()
     moms = spins.shape[0]
@@ -128,8 +128,8 @@
     def elementals(rows, m):
         return jnp.concatenate([rows[:, (2 * m + h) * 128 : (2 * m + h + 1) * 128] for h in range(2)], axis=0)
 
-    mine = mine_ref[width : width + 64, :]
-    other = joined(others)[width : width + 64, :]
+    mine = mine_ref[0:64, :]
+    other = first[0:64, :]
 
     lefts = []
     for m in range(moms):
@@ -169,7 +169,7 @@
     return pl.pallas_call(
         mixed_kernel,
         out_shape=jax.ShapeDtypeStruct((ops, 2, rows, width), bf16),
-        in_specs=[pl.BlockSpec(memory_space=pl.ANY)] + [vmem_spec] * (2 + len(other)),
+        in_specs=[pl.BlockSpec(memory_space=pl.ANY)] + [vmem_spec] * 3,
         out_specs=vmem_spec,
         scratch_shapes=[
             pltpu.VMEM((moms, 4, 4, 128, width), bf16),
@@ -179,7 +179,7 @@
         compiler_params=pltpu.CompilerParams(vmem_limit_bytes=LIMIT),
         cost_estimate=pl.CostEstimate(flops=1, bytes_accessed=1, transcendentals=0),
         name="mixed",
-    )(picks, mine, *other, prop)
+    )(picks, mine, other, prop)
 
 
 def block_kernel(places, cols, counts, *refs):
@@ -195,7 +195,7 @@
         mixed = mixes[slot]
         ops, width = mixed.shape[0], mixed.shape[3]
         source = lax.rem(lax.axis_index("col") + hop, cols)
-        ours, theirs = mine[0:width, :], joined(others)[0:width, :]
+        ours, theirs = mine[mine.shape[0] - width :, :], joined(others)[-width:, :]
         sinks = [
             jnp.concatenate([ours, theirs], axis=1),
             jnp.concatenate([jnp.where(part == 0, ours, -ours), jnp.where(part == 0, -theirs, theirs)], axis=1),
@@ -337,15 +337,15 @@
             first, second = [lax.ppermute(block, "tm", later) for block in moving]
             *props, picks = fetch(op_mom, op_gamma, prop_src)
             first, props, picks = lax.optimization_barrier((first, props, picks))
-            held = jnp.concatenate([first, second])
+            held = jnp.concatenate([second, first])
         else:
             held, out = lax.optimization_barrier((lax.ppermute(held, "tm", later), out))
-        other = swapped(held, (6,) if slot == 0 else (6,))
+        other = swapped(held, (10,) if slot == 0 else (14,))
         arrivals = [
-            (slot, hop, lax.ppermute(held[:width], "col", [((i + hop) % cols, i) for i in range(cols)]))
+            (slot, hop, lax.ppermute(held[-width:], "col", [((i + hop) % cols, i) for i in range(cols)]))
             for hop in range(1, cols)
         ]
-        mixes[slot] = mixed_blocks(picks, held, other, props[slot])
+        mixes[slot] = mixed_blocks(picks, held, other[0], props[slot])
         out = blocks(cols, waiting + [(slot, 0, held, other)], mixes, out, out_shape)
         waiting = []
         for place, hop, mine in arrivals:

time: 35.5 us -> 35.1 us (0.989)
  waiting for transfers between devices: 5.63 us -> 4.94 us
  starting transfers between devices: 14.4 us -> 14.8 us
    ppermute x7, waiting for transfers between devices: 2.55 us -> 1.93 us  [swapped(): lax.ppermute(block[i:j], 'mom', swap)]
    ppermute x7, starting transfers between devices: 1.44 us -> 1.82 us  [swapped(): lax.ppermute(block[i:j], 'mom', swap)]
  transfers between devices with their start and end apart: 12 -> 12, of which waited for: 7 -> 6; matrix products, arithmetic and copies ran while one was open for 0% -> 0% of each run, Pallas kernels for 25% -> 25%
where the time goes in v1:
time: 35.1 us; the launch traced here: 34.9 us
  starting transfers between devices  14.8 us (42%)
  Pallas kernels  10.4 us (30%)
  waiting for transfers between devices  4.94 us (14%)
  local copies, waits for them, and re-layouts  4.59 us (13%)
    ppermute x2, starting transfers between devices, on_device(): first, second = [lax.ppermute(block, 'tm', later) for block in moving]  5.6 us
    pallas_call x2, Pallas kernels, blocks(): pl.pallas_call(functools.partial(block_kernel, places, cols, [len(others)...  5.24 us
    unnamed x11, local copies, waits for them, and re-layouts  4.48 us
    ppermute x1, starting transfers between devices, on_device(): held, out = lax.optimization_barrier((lax.ppermute(held, 'tm', later), out))  4.33 us
    ppermute x2, starting transfers between devices, on_device(): lax.ppermute(held[-width:], 'col', [((i + hop) % cols, i) for i in range(...  3.05 us
    ppermute x7, waiting for transfers between devices, swapped(): lax.ppermute(block[i:j], 'mom', swap)  1.93 us
    ppermute x7, starting transfers between devices, swapped(): lax.ppermute(block[i:j], 'mom', swap)  1.82 us
    ppermute x2, waiting for transfers between devices, on_device(): first, second = [lax.ppermute(block, 'tm', later) for block in moving]  1.65 us
  transfers between devices with their start and end apart: 12, of which 6 were waited for; matrix products, arithmetic and copies ran while one was open for 0% of the time, Pallas kernels for 25%

profile of v1, /device:TPU:0, one launch (start us, length us, event | category | flops | bytes accessed | tf_op | source)
XLA Modules:
  0.0 34.9 jit_solution(3928790868164101284)
XLA Ops:
  0.0 0.0 copy-start.1
  0.0 1.0 %copy-done.1 = bf16[1,2,512,256]{3,2,1,0:T(8,128)(2,1)S(1)} copy-done((bf16[1,2,512,256]{3,2,1,0:T(8,128)(2,1)S(1)}, bf16[1,2,512,256]{3,2,1,0:T(8,128)(2,1)}, u32[]{:S(2)}) %copy-start.1) | copy-done | bytes 524312
  1.0 0.1 turned.1.after_ref
  1.2 5.1 %collective-permute-start.1 = (bf16[256,512]{1,0:T(8,128)(2,1)S(1)}, bf16[256,512]{1,0:T(8,128)(2,1)S(1)}, u32[]{:S(2)}, u32[]{:S(2)}) collective-permute-start(bf16[256,512]{1,0:T(8,128)(2,1)S(1)} %turned.1.after_ref), channel_id=1, source_target_pairs={{4,0},{8,4},{12,8},{0,12},{5,1},{9,5},{13,9},{1,13},{6,2},{10,6},{... | collective-permute-start | bytes 786440 | tf_op jit(solution)/shard_map/ppermute | solution.py:337
  6.3 0.0 copy-start.2
  6.3 0.9 %copy-done.2 = bf16[1,2,2,128,128]{4,3,2,1,0:T(8,128)(2,1)S(1)} copy-done((bf16[1,2,2,128,128]{4,3,2,1,0:T(8,128)(2,1)S(1)}, bf16[1,2,2,128,128]{4,3,2,1,0:T(8,128)(2,1)}, u32[]{:S(2)}) %copy-start.2) | copy-done | bytes 131096
  7.2 0.1 laid.1
  7.3 0.5 %collective-permute-start = (bf16[64,512]{1,0:T(8,128)(2,1)S(1)}, bf16[64,512]{1,0:T(8,128)(2,1)S(1)}, u32[]{:S(2)}, u32[]{:S(2)}) collective-permute-start(bf16[64,512]{1,0:T(8,128)(2,1)S(1)} %laid.1), channel_id=1, source_target_pairs={{4,0},{8,4},{12,8},{0,12},{5,1},{9,5},{13,9},{1,13},{6,2},{10,6},{... | collective-permute-start | bytes 196616 | tf_op jit(solution)/shard_map/ppermute | solution.py:337
  7.8 0.0 copy-start
  7.8 1.2 %copy-done = bf16[1,2,2,512,256]{4,3,2,1,0:T(8,128)(2,1)S(1)} copy-done((bf16[1,2,2,512,256]{4,3,2,1,0:T(8,128)(2,1)S(1)}, bf16[1,2,2,512,256]{4,3,2,1,0:T(8,128)(2,1)}, u32[]{:S(2)}) %copy-start) | copy-done | bytes 1048600
  9.0 0.0 copy-start.3
  9.0 0.7 %copy-done.3 = s32[4]{0:T(128)S(1)} copy-done((s32[4]{0:T(128)S(1)}, s32[4]{0:T(128)}, u32[]{:S(2)}) %copy-start.3) | copy-done | bytes 40
  9.7 0.0 copy-start.4
  9.7 0.7 %copy-done.4 = s32[4]{0:T(128)S(1)} copy-done((s32[4]{0:T(128)S(1)}, s32[4]{0:T(128)}, u32[]{:S(2)}) %copy-start.4) | copy-done | bytes 40
  10.3 1.3 %fetch.1 = (bf16[2,512,256]{2,1,0:T(8,128)(2,1)S(1)}, bf16[2,512,256]{2,1,0:T(8,128)(2,1)S(1)}, s32[2,4]{1,0:T(2,128)S(1)}) custom-call(s32[4]{0:T(128)S(1)} %copy-done.3, s32[4]{0:T(128)S(1)} %copy-done.4, bf16[1,2,2,512,256]{4,3,2,1,0:T(8,128)(2,1)S(1)} %copy-done), custom_call_target="tpu_custom_call" | custom-call | tf_op jit(solution)/shard_map/fetch/pallas_call | solution.py:105
  11.6 1.7 %collective-permute-done = bf16[64,512]{1,0:T(8,128)(2,1)S(1)} collective-permute-done((bf16[64,512]{1,0:T(8,128)(2,1)S(1)}, bf16[64,512]{1,0:T(8,128)(2,1)S(1)}, u32[]{:S(2)}, u32[]{:S(2)}) %collective-permute-start) | collective-permute-done | bytes 65568 | tf_op jit(solution)/shard_map/ppermute | solution.py:337
  13.3 0.0 collective-permute-done.1
  13.3 4.3 %collective-permute-start.2 = (bf16[320,512]{1,0:T(8,128)(2,1)S(1)}, bf16[320,512]{1,0:T(8,128)(2,1)S(1)}, u32[]{:S(2)}, u32[]{:S(2)}) collective-permute-start(bf16[320,512]{1,0:T(8,128)(2,1)S(1)} %constant_dynamic-update-slice_fusion.mine_ref.refs_0_), channel_id=1, source_target_pairs={{4,0},{8,4},{12,8},{0,12},{5,1},{9,5},{13,9},{1,13},{6,2},{10,6},{... | collective-permute-start | bytes 983048 | tf_op jit(solution)/shard_map/ppermute | solution.py:342
  17.6 1.5 %collective-permute-start.6 = (bf16[256,512]{1,0:T(8,128)(2,1)S(1)}, bf16[256,512]{1,0:T(8,128)(2,1)S(1)}, u32[]{:S(2)}, u32[]{:S(2)}) collective-permute-start(bf16[256,512]{1,0:T(8,128)(2,1)S(1)} %collective-permute-done.1), channel_id=1, source_target_pairs={{2,0},{0,2},{3,1},{1,3},{6,4},{4,6},{7,5},{5,7},{10,8},{8,10},{11,... | collective-permute-start | bytes 786440 | tf_op jit(solution)/shard_map/ppermute | solution.py:345
  19.1 0.1 collective-permute-start.3
  19.2 0.6 %collective-permute-start.4 = (bf16[160,512]{1,0:T(8,128)(2,1)S(1)}, bf16[160,512]{1,0:T(8,128)(2,1)S(1)}, u32[]{:S(2)}, u32[]{:S(2)}) collective-permute-start(bf16[160,512]{1,0:T(8,128)(2,1)S(1)} %slice.22), channel_id=1, source_target_pairs={{0,1},{1,0},{2,3},{3,2},{4,5},{5,4},{6,7},{7,6},{8,9},{9,8},{10,11... | collective-permute-start | bytes 491528 | tf_op jit(solution)/shard_map/ppermute | solution.py:328
  19.8 0.8 %collective-permute-done.3.refs_0_.refs_1_ = bf16[160,512]{1,0:T(8,128)(2,1)S(1)} collective-permute-done((bf16[160,512]{1,0:T(8,128)(2,1)S(1)}, bf16[160,512]{1,0:T(8,128)(2,1)S(1)}, u32[]{:S(2)}, u32[]{:S(2)}) %collective-permute-start.3) | collective-permute-done | bytes 163872 | tf_op jit(solution)/shard_map/ppermute | solution.py:328
  20.6 0.7 %mixed.2.refs_3_.refs_6_ = bf16[4,2,512,256]{3,2,1,0:T(8,128)(2,1)S(1)} custom-call(s32[2,4]{1,0:T(2,128)S(1)} %get-tuple-element.20.picks, bf16[320,512]{1,0:T(8,128)(2,1)S(1)} %constant_dynamic-update-slice_fusion.mine_ref.refs_0_, bf16[160,512]{1,0:T(8,128)(2,1)S(1)} %collective-permute-done.3.refs_0_.refs_1_, ...), custom_call_target="tpu_custom_call" | custom-call | flops 1 | bytes 1 | tf_op jit(solution)/shard_map/mixed/pallas_call | solution.py:169
  21.3 0.0 collective-permute-done.4.refs_2_
  21.3 2.0 %blocks.2.refs_8_ = bf16[1,2,4,2,512,256]{5,4,3,2,1,0:T(8,128)(2,1)} custom-call(bf16[320,512]{1,0:T(8,128)(2,1)S(1)} %constant_dynamic-update-slice_fusion.mine_ref.refs_0_, bf16[160,512]{1,0:T(8,128)(2,1)S(1)} %collective-permute-done.3.refs_0_.refs_1_, bf16[160,512]{1,0:T(8,128)(2,1)S(1)} %collective-permute-done.4.refs_2_, ...), custom_call_target="tpu_custom_call" | custom-call | flops 1 | bytes 1 | tf_op jit(solution)/shard_map/blocks/pallas_call | solution.py:233
  23.4 0.4 %collective-permute-done.2.mine_ref.refs_3_ = bf16[320,512]{1,0:T(8,128)(2,1)S(1)} collective-permute-done((bf16[320,512]{1,0:T(8,128)(2,1)S(1)}, bf16[320,512]{1,0:T(8,128)(2,1)S(1)}, u32[]{:S(2)}, u32[]{:S(2)}) %collective-permute-start.2) | collective-permute-done | bytes 327712 | tf_op jit(solution)/shard_map/ppermute | solution.py:342
  23.8 1.6 %collective-permute-start.5 = (bf16[256,512]{1,0:T(8,128)(2,1)S(1)}, bf16[256,512]{1,0:T(8,128)(2,1)S(1)}, u32[]{:S(2)}, u32[]{:S(2)}) collective-permute-start(bf16[256,512]{1,0:T(8,128)(2,1)S(1)} %slice.23), channel_id=1, source_target_pairs={{2,0},{0,2},{3,1},{1,3},{6,4},{4,6},{7,5},{5,7},{10,8},{8,10},{11,... | collective-permute-start | bytes 786440 | tf_op jit(solution)/shard_map/ppermute | solution.py:345
  25.3 0.1 collective-permute-start.9
  25.4 0.0 collective-permute-done.6.refs_0_
  25.5 0.6 %collective-permute-start.8 = (bf16[192,512]{1,0:T(8,128)(2,1)S(1)}, bf16[192,512]{1,0:T(8,128)(2,1)S(1)}, u32[]{:S(2)}, u32[]{:S(2)}) collective-permute-start(bf16[192,512]{1,0:T(8,128)(2,1)S(1)} %slice.30), channel_id=1, source_target_pairs={{0,1},{1,0},{2,3},{3,2},{4,5},{5,4},{6,7},{7,6},{8,9},{9,8},{10,11... | collective-permute-start | bytes 589832 | tf_op jit(solution)/shard_map/ppermute | solution.py:328
  26.0 0.1 collective-permute-start.10
  26.1 0.5 %collective-permute-start.7 = (bf16[64,512]{1,0:T(8,128)(2,1)S(1)}, bf16[64,512]{1,0:T(8,128)(2,1)S(1)}, u32[]{:S(2)}, u32[]{:S(2)}) collective-permute-start(bf16[64,512]{1,0:T(8,128)(2,1)S(1)} %slice.29), channel_id=1, source_target_pairs={{0,1},{1,0},{2,3},{3,2},{4,5},{5,4},{6,7},{7,6},{8,9},{9,8},{10,11... | collective-permute-start | bytes 196616 | tf_op jit(solution)/shard_map/ppermute | solution.py:328
  26.6 0.3 collective-permute-done.9.refs_0_.refs_4_
  26.9 0.7 %mixed.3.refs_7_.refs_1_ = bf16[4,2,512,256]{3,2,1,0:T(8,128)(2,1)S(1)} custom-call(s32[2,4]{1,0:T(2,128)S(1)} %get-tuple-element.20.picks, bf16[320,512]{1,0:T(8,128)(2,1)S(1)} %collective-permute-done.2.mine_ref.refs_3_, bf16[224,512]{1,0:T(8,128)(2,1)S(1)} %collective-permute-done.9.refs_0_.refs_4_, bf16[2,512,256]{2,1,0:T(8,128)(2,1)S(1)} %get-tuple-element.23.refs_1_), custom_call_target="tpu_custom_call" | custom-call | flops 1 | bytes 1 | tf_op jit(solution)/shard_map/mixed/pallas_call | solution.py:169
  27.6 0.0 collective-permute-done.7.refs_1_
  27.6 0.0 collective-permute-done.10.refs_5_
  27.6 0.0 collective-permute-done.8.refs_2_
  27.6 3.2 %blocks.3.refs_3_ = bf16[1,2,4,2,512,256]{5,4,3,2,1,0:T(8,128)(2,1)} custom-call(bf16[256,512]{1,0:T(8,128)(2,1)S(1)} %collective-permute-done.6.refs_0_, bf16[64,512]{1,0:T(8,128)(2,1)S(1)} %collective-permute-done.7.refs_1_, bf16[192,512]{1,0:T(8,128)(2,1)S(1)} %collective-permute-done.8.refs_2_, ...), custom_call_target="tpu_custom_call", output_to_operand_aliasing={{}: (8, {})} | custom-call | flops 1 | bytes 1 | tf_op jit(solution)/shard_map/blocks/pallas_call | solution.py:233
  30.9 1.0 %collective-permute-done.5.mine_ref = bf16[256,512]{1,0:T(8,128)(2,1)S(1)} collective-permute-done((bf16[256,512]{1,0:T(8,128)(2,1)S(1)}, bf16[256,512]{1,0:T(8,128)(2,1)S(1)}, u32[]{:S(2)}, u32[]{:S(2)}) %collective-permute-start.5) | collective-permute-done | bytes 262176 | tf_op jit(solution)/shard_map/ppermute | solution.py:345
  31.9 0.0 collective-permute-start.11
  31.9 0.7 %half.1.refs_2_ = f32[4,2,256,256]{3,2,1,0:T(8,128)S(1)} custom-call(bf16[256,512]{1,0:T(8,128)(2,1)S(1)} %collective-permute-done.5.mine_ref, bf16[4,2,512,256]{3,2,1,0:T(8,128)(2,1)S(1)} %mixed.3.refs_7_.refs_1_), custom_call_target="tpu_custom_call" | custom-call | flops 1 | bytes 1 | tf_op jit(solution)/shard_map/half/pallas_call | solution.py:265
  32.6 0.8 %collective-permute-done.11.refs_0_ = bf16[256,512]{1,0:T(8,128)(2,1)S(1)} collective-permute-done((bf16[256,512]{1,0:T(8,128)(2,1)S(1)}, bf16[256,512]{1,0:T(8,128)(2,1)S(1)}, u32[]{:S(2)}, u32[]{:S(2)}) %collective-permute-start.11) | collective-permute-done | bytes 262176 | tf_op jit(solution)/shard_map/ppermute | solution.py:328
  33.4 1.5 %rest.1 = bf16[1,2,4,2,512,256]{5,4,3,2,1,0:T(8,128)(2,1)} custom-call(bf16[256,512]{1,0:T(8,128)(2,1)S(1)} %collective-permute-done.11.refs_0_, bf16[4,2,512,256]{3,2,1,0:T(8,128)(2,1)S(1)} %mixed.3.refs_7_.refs_1_, f32[4,2,256,256]{3,2,1,0:T(8,128)S(1)} %half.1.refs_2_, bf16[1,2,4,2,512,256]{5,4,3,2,1,0:T(8,128)(2,1)} %blocks.3.refs_3_), custom_call_target="tpu_custom_call", output_to_operand_aliasing={{}: (3, {})} | custom-call | flops 1 | bytes 1 | tf_op jit(solution)/shard_map/rest/pallas_call | solution.py:303
  (9 shorter events, 0.1 us)
Async XLA Ops:
  0.0 1.0 %copy-start.1 = (bf16[1,2,512,256]{3,2,1,0:T(8,128)(2,1)S(1)}, bf16[1,2,512,256]{3,2,1,0:T(8,128)(2,1)}, u32[]{:S(2)}) copy-start(bf16[1,2,512,256]{3,2,1,0:T(8,128)(2,1)} %sink_ref.1) | copy-start | bytes 1572868
  1.2 12.1 %collective-permute-start.1 = (bf16[256,512]{1,0:T(8,128)(2,1)S(1)}, bf16[256,512]{1,0:T(8,128)(2,1)S(1)}, u32[]{:S(2)}, u32[]{:S(2)}) collective-permute-start(bf16[256,512]{1,0:T(8,128)(2,1)S(1)} %turned.1.after_ref), channel_id=1, source_target_pairs={{4,0},{8,4},{12,8},{0,12},{5,1},{9,5},{13,9},{1,13},{6,2},{10,6},{... | collective-permute-start | bytes 786440 | tf_op jit(solution)/shard_map/ppermute | solution.py:337
  6.3 0.9 %copy-start.2 = (bf16[1,2,2,128,128]{4,3,2,1,0:T(8,128)(2,1)S(1)}, bf16[1,2,2,128,128]{4,3,2,1,0:T(8,128)(2,1)}, u32[]{:S(2)}) copy-start(bf16[1,2,2,128,128]{4,3,2,1,0:T(8,128)(2,1)} %elem_ref.1) | copy-start | bytes 393220
  7.3 6.0 %collective-permute-start = (bf16[64,512]{1,0:T(8,128)(2,1)S(1)}, bf16[64,512]{1,0:T(8,128)(2,1)S(1)}, u32[]{:S(2)}, u32[]{:S(2)}) collective-permute-start(bf16[64,512]{1,0:T(8,128)(2,1)S(1)} %laid.1), channel_id=1, source_target_pairs={{4,0},{8,4},{12,8},{0,12},{5,1},{9,5},{13,9},{1,13},{6,2},{10,6},{... | collective-permute-start | bytes 196616 | tf_op jit(solution)/shard_map/ppermute | solution.py:337
  7.8 1.2 %copy-start = (bf16[1,2,2,512,256]{4,3,2,1,0:T(8,128)(2,1)S(1)}, bf16[1,2,2,512,256]{4,3,2,1,0:T(8,128)(2,1)}, u32[]{:S(2)}) copy-start(bf16[1,2,2,512,256]{4,3,2,1,0:T(8,128)(2,1)} %prop_ref.1) | copy-start | bytes 3145732
  9.0 0.7 %copy-start.3 = (s32[4]{0:T(128)S(1)}, s32[4]{0:T(128)}, u32[]{:S(2)}) copy-start(s32[4]{0:T(128)} %mom_ref.1) | copy-start | bytes 52
  9.7 0.7 %copy-start.4 = (s32[4]{0:T(128)S(1)}, s32[4]{0:T(128)}, u32[]{:S(2)}) copy-start(s32[4]{0:T(128)} %gamma_ref.1) | copy-start | bytes 52
  13.3 10.4 %collective-permute-start.2 = (bf16[320,512]{1,0:T(8,128)(2,1)S(1)}, bf16[320,512]{1,0:T(8,128)(2,1)S(1)}, u32[]{:S(2)}, u32[]{:S(2)}) collective-permute-start(bf16[320,512]{1,0:T(8,128)(2,1)S(1)} %constant_dynamic-update-slice_fusion.mine_ref.refs_0_), channel_id=1, source_target_pairs={{4,0},{8,4},{12,8},{0,12},{5,1},{9,5},{13,9},{1,13},{6,2},{10,6},{... | collective-permute-start | bytes 983048 | tf_op jit(solution)/shard_map/ppermute | solution.py:342
  17.6 7.8 %collective-permute-start.6 = (bf16[256,512]{1,0:T(8,128)(2,1)S(1)}, bf16[256,512]{1,0:T(8,128)(2,1)S(1)}, u32[]{:S(2)}, u32[]{:S(2)}) collective-permute-start(bf16[256,512]{1,0:T(8,128)(2,1)S(1)} %collective-permute-done.1), channel_id=1, source_target_pairs={{2,0},{0,2},{3,1},{1,3},{6,4},{4,6},{7,5},{5,7},{10,8},{8,10},{11,... | collective-permute-start | bytes 786440 | tf_op jit(solution)/shard_map/ppermute | solution.py:345
  19.1 1.5 %collective-permute-start.3 = (bf16[160,512]{1,0:T(8,128)(2,1)S(1)}, bf16[160,512]{1,0:T(8,128)(2,1)S(1)}, u32[]{:S(2)}, u32[]{:S(2)}) collective-permute-start(bf16[160,512]{1,0:T(8,128)(2,1)S(1)} %slice.28), channel_id=1, source_target_pairs={{0,1},{1,0},{2,3},{3,2},{4,5},{5,4},{6,7},{7,6},{8,9},{9,8},{10,11... | collective-permute-start | bytes 491528 | tf_op jit(solution)/shard_map/ppermute | solution.py:328
  19.2 2.1 %collective-permute-start.4 = (bf16[160,512]{1,0:T(8,128)(2,1)S(1)}, bf16[160,512]{1,0:T(8,128)(2,1)S(1)}, u32[]{:S(2)}, u32[]{:S(2)}) collective-permute-start(bf16[160,512]{1,0:T(8,128)(2,1)S(1)} %slice.22), channel_id=1, source_target_pairs={{0,1},{1,0},{2,3},{3,2},{4,5},{5,4},{6,7},{7,6},{8,9},{9,8},{10,11... | collective-permute-start | bytes 491528 | tf_op jit(solution)/shard_map/ppermute | solution.py:328
  23.8 8.1 %collective-permute-start.5 = (bf16[256,512]{1,0:T(8,128)(2,1)S(1)}, bf16[256,512]{1,0:T(8,128)(2,1)S(1)}, u32[]{:S(2)}, u32[]{:S(2)}) collective-permute-start(bf16[256,512]{1,0:T(8,128)(2,1)S(1)} %slice.23), channel_id=1, source_target_pairs={{2,0},{0,2},{3,1},{1,3},{6,4},{4,6},{7,5},{5,7},{10,8},{8,10},{11,... | collective-permute-start | bytes 786440 | tf_op jit(solution)/shard_map/ppermute | solution.py:345
  25.3 1.6 %collective-permute-start.9 = (bf16[224,512]{1,0:T(8,128)(2,1)S(1)}, bf16[224,512]{1,0:T(8,128)(2,1)S(1)}, u32[]{:S(2)}, u32[]{:S(2)}) collective-permute-start(bf16[224,512]{1,0:T(8,128)(2,1)S(1)} %slice.26), channel_id=1, source_target_pairs={{0,1},{1,0},{2,3},{3,2},{4,5},{5,4},{6,7},{7,6},{8,9},{9,8},{10,11... | collective-permute-start | bytes 688136 | tf_op jit(solution)/shard_map/ppermute | solution.py:328
  25.5 2.2 %collective-permute-start.8 = (bf16[192,512]{1,0:T(8,128)(2,1)S(1)}, bf16[192,512]{1,0:T(8,128)(2,1)S(1)}, u32[]{:S(2)}, u32[]{:S(2)}) collective-permute-start(bf16[192,512]{1,0:T(8,128)(2,1)S(1)} %slice.30), channel_id=1, source_target_pairs={{0,1},{1,0},{2,3},{3,2},{4,5},{5,4},{6,7},{7,6},{8,9},{9,8},{10,11... | collective-permute-start | bytes 589832 | tf_op jit(solution)/shard_map/ppermute | solution.py:328
  26.0 1.6 %collective-permute-start.10 = (bf16[96,512]{1,0:T(8,128)(2,1)S(1)}, bf16[96,512]{1,0:T(8,128)(2,1)S(1)}, u32[]{:S(2)}, u32[]{:S(2)}) collective-permute-start(bf16[96,512]{1,0:T(8,128)(2,1)S(1)} %slice.27), channel_id=1, source_target_pairs={{0,1},{1,0},{2,3},{3,2},{4,5},{5,4},{6,7},{7,6},{8,9},{9,8},{10,11... | collective-permute-start | bytes 294920 | tf_op jit(solution)/shard_map/ppermute | solution.py:328
  26.1 1.5 %collective-permute-start.7 = (bf16[64,512]{1,0:T(8,128)(2,1)S(1)}, bf16[64,512]{1,0:T(8,128)(2,1)S(1)}, u32[]{:S(2)}, u32[]{:S(2)}) collective-permute-start(bf16[64,512]{1,0:T(8,128)(2,1)S(1)} %slice.29), channel_id=1, source_target_pairs={{0,1},{1,0},{2,3},{3,2},{4,5},{5,4},{6,7},{7,6},{8,9},{9,8},{10,11... | collective-permute-start | bytes 196616 | tf_op jit(solution)/shard_map/ppermute | solution.py:328
  31.9 1.5 %collective-permute-start.11 = (bf16[256,512]{1,0:T(8,128)(2,1)S(1)}, bf16[256,512]{1,0:T(8,128)(2,1)S(1)}, u32[]{:S(2)}, u32[]{:S(2)}) collective-permute-start(bf16[256,512]{1,0:T(8,128)(2,1)S(1)} %collective-permute-done.5.mine_ref), channel_id=1, source_target_pairs={{0,1},{1,0},{2,3},{3,2},{4,5},{5,4},{6,7},{7,6},{8,9},{9,8},{10,11... | collective-permute-start | bytes 786440 | tf_op jit(solution)/shard_map/ppermute | solution.py:328
